TPU v7x, 256 devices: a whole 4x4x8 slice. The times are simulated.
256 devices in a mesh: row: 8 (over y, z_hi), col: 32 (over x, z_lo, core).
Axes of the slice: x: 4, y: 4, z: 8 (z_hi: 2, z_lo: 4; z = z_hi * 4 + z_lo), core: 2. Of those that a mesh axis runs over, the one named last changes fastest.
Arguments:
- a_values: bfloat16 [2, 12288, 4096], P(None, 'row', 'col'), may hold values from -0.44140625 to 0.44140625
- a_pattern: int32 [2, 96, 32], P(None, 'row', 'col'), may hold values 0 or 1
- c_mask: int32 [96, 96], P('row', 'col'), may hold values 0 or 1
Outputs:
- scores: float32 [12288, 12288], P('row', 'col')
All inputs are finite; a program needn't handle non-finite values. No bound on the sum of `a_pattern` or of `c_mask` on one device may be relied on, other than what follows from the above.
Results may differ from a plain program's by a relative error of at most 0.0003.
Values may be sent and summed in bfloat16 or wider, within the bound.
A program may use at most 128 MiB of HBM per device.

v0:
```python
import jax
import jax.numpy as jnp
from jax import lax
from jax.sharding import PartitionSpec as P

TILE = 128
SECTIONS = 2


def spread_tiles(pattern):
    grown = jnp.repeat(pattern, TILE, axis=-2)
    return jnp.repeat(grown, TILE, axis=-1)


def product_nt(left, right):
    return lax.dot_general(
        left, right, (((1,), (1,)), ((), ())), preferred_element_type=jnp.float32
    )


def shards(a_values, a_pattern, c_mask):
    live_tiles = a_values * spread_tiles(a_pattern).astype(jnp.bfloat16)
    row_count = live_tiles.shape[1]
    col_width = c_mask.shape[1] * TILE
    total = jnp.zeros((row_count, col_width), jnp.float32)
    for section in range(SECTIONS):
        local_panel = live_tiles[section]
        all_pages = lax.all_gather(local_panel, "row", axis=0, tiled=True)
        column_block = lax.all_to_all(all_pages, "col", split_axis=0, concat_axis=1, tiled=True)
        total = total + product_nt(
            lax.all_gather(local_panel, "col", axis=1, tiled=True), column_block
        )
    return total * spread_tiles(c_mask).astype(jnp.float32)


def solution(mesh):
    return jax.shard_map(
        shards,
        mesh=mesh,
        in_specs=(P(None, "row", "col"), P(None, "row", "col"), P("row", "col")),
        out_specs=P("row", "col"),
        check_vma=False,
    )
```

profile of v0, /device:TPU:1, one launch (start us, length us, event | category | flops | bytes accessed | tf_op | source)
XLA Modules:
  0.0 498.5 jit_solution(13141279547738618645)
XLA Ops:
  6.5 0.0 all-gather.15.cloned.1.call-start
  6.5 0.7 convert_element_type.22
  7.2 0.1 broadcast_bitcast_fusion.1
  7.3 1.6 broadcast_multiply_fusion
  8.9 1.0 fusion.10
  9.9 0.0 all-gather.15.cloned.1.call-update
  9.9 0.0 all-gather.11.cloned.1.call-start
  10.0 0.7 all-gather.11.cloned.1.call-update
  10.7 0.0 all-gather.13.cloned.1.call-start
  10.7 0.7 all-gather.13.cloned.1.call-update
  11.4 0.0 all-gather.9.cloned.1.call-start
  11.4 0.5 all-gather.9.cloned.1.call-update
  12.0 93.3 %all-gather.15.cloned.1.call-done = bf16[1,12288,128]{2,1,0:T(8,128)(2,1)} async-done(((bf16[1,1536,128]{2,1,0:T(8,128)(2,1)}), bf16[1,12288,128]{2,1,0:T(8,128)(2,1)}) %all-gather.15.cloned.1.call-update) | async-done | bytes 3145744 | tf_op jit(solution)/shard_map/all_gather | solution.py:28
  105.3 5.6 %all-to-all-start.1 = ((bf16[32,384,128]{2,1,0:T(8,128)(2,1)}), bf16[32,384,128]{2,1,0:T(8,128)(2,1)S(1)}, u32[]{:S(2)}, u32[]{:S(2)}) async-start(bf16[32,384,128]{2,1,0:T(8,128)(2,1)} %bitcast.37), calls=%async_computation.1 | async-start | bytes 6291456 | tf_op jit(solution)/shard_map/all_to_all | solution.py:29
  110.9 104.5 %all-gather.11.cloned.1.call-done = bf16[1,12288,128]{2,1,0:T(8,128)(2,1)} async-done(((bf16[1,1536,128]{2,1,0:T(8,128)(2,1)}), bf16[1,12288,128]{2,1,0:T(8,128)(2,1)}) %all-gather.11.cloned.1.call-update) | async-done | bytes 3145744 | tf_op jit(solution)/shard_map/all_gather | solution.py:28
  215.4 9.6 %all-to-all-done.1 = bf16[32,384,128]{2,1,0:T(8,128)(2,1)S(1)} async-done(((bf16[32,384,128]{2,1,0:T(8,128)(2,1)}), bf16[32,384,128]{2,1,0:T(8,128)(2,1)S(1)}, u32[]{:S(2)}, u32[]{:S(2)}) %all-to-all-start.1) | async-done | bytes 3145760 | tf_op jit(solution)/shard_map/all_to_all | solution.py:29
  225.0 0.0 copy-start
  225.0 5.8 %all-to-all-start = ((bf16[32,384,128]{2,1,0:T(8,128)(2,1)}), bf16[32,384,128]{2,1,0:T(8,128)(2,1)}, u32[]{:S(2)}, u32[]{:S(2)}) async-start(bf16[32,384,128]{2,1,0:T(8,128)(2,1)} %bitcast.36), calls=%async_computation | async-start | bytes 6291456 | tf_op jit(solution)/shard_map/all_to_all | solution.py:29
  230.8 0.0 copy-done
  230.8 0.1 broadcast_bitcast_fusion
  230.9 1.7 broadcast_in_dim.12
  232.6 3.1 copy.8
  235.7 2.8 copy.7
  238.5 95.2 %all-to-all-done = bf16[32,384,128]{2,1,0:T(8,128)(2,1)} async-done(((bf16[32,384,128]{2,1,0:T(8,128)(2,1)}), bf16[32,384,128]{2,1,0:T(8,128)(2,1)}, u32[]{:S(2)}, u32[]{:S(2)}) %all-to-all-start) | async-done | bytes 3145760 | tf_op jit(solution)/shard_map/all_to_all | solution.py:29
  333.7 3.4 copy.6
  337.1 37.2 %all-gather.13.cloned.1.call-done = bf16[1,1536,4096]{2,1,0:T(8,128)(2,1)} async-done(((bf16[1,1536,128]{2,1,0:T(8,128)(2,1)}), bf16[1,1536,4096]{2,1,0:T(8,128)(2,1)}) %all-gather.13.cloned.1.call-update) | async-done | bytes 12582928 | tf_op jit(solution)/shard_map/all_gather | solution.py:31
  374.3 11.6 %fusion = f32[1536,384]{1,0:T(8,128)} fusion(bf16[384,4096]{0,1:T(8,128)(2,1)} %bitcast.39, bf16[1,1536,4096]{2,1,0:T(8,128)(2,1)} %all-gather.13.cloned.1.call-done), kind=kOutput, calls=%fused_computation | convolution fusion | flops 4831838208 | bytes 18087936 | tf_op jit(solution)/shard_map/dot_general | solution.py:16
  386.0 94.7 %all-gather.9.cloned.1.call-done = bf16[1,1536,4096]{2,1,0:T(8,128)(2,1)} async-done(((bf16[1,1536,128]{2,1,0:T(8,128)(2,1)}), bf16[1,1536,4096]{2,1,0:T(8,128)(2,1)}) %all-gather.9.cloned.1.call-update) | async-done | bytes 12582928 | tf_op jit(solution)/shard_map/all_gather | solution.py:31
  480.6 11.3 %fusion.7 = f32[1536,384]{1,0:T(8,128)} fusion(f32[1536,384]{1,0:T(8,128)} %copy.8, f32[1536,384]{1,0:T(8,128)} %fusion, bf16[384,4096]{0,1:T(8,128)(2,1)S(1)} %bitcast.38, bf16[1,1536,4096]{2,1,0:T(8,128)(2,1)} %all-gather.9.cloned.1.call-done), kind=kOutput, calls=%fused_computation.5 | convolution fusion | flops 4833017856 | bytes 22806528 | tf_op jit(solution)/shard_map/dot_general | solution.py:16
  (4 shorter events, 0.0 us)
Async XLA Ops:
  6.5 98.8 %all-gather.15.cloned.1.call-start = ((), (), s32[]{:S(2)}) async-start(), calls=%async_computation.5 | async-start | bytes 3538944 | tf_op jit(solution)/shard_map/all_gather | solution.py:28
  9.9 205.5 %all-gather.11.cloned.1.call-start = ((), (), s32[]{:S(2)}) async-start(), calls=%async_computation.3 | async-start | bytes 3538944 | tf_op jit(solution)/shard_map/all_gather | solution.py:28
  10.7 363.7 %all-gather.13.cloned.1.call-start = ((), (), s32[]{:S(2)}) async-start(), calls=%async_computation.4 | async-start | bytes 12976128 | tf_op jit(solution)/shard_map/all_gather | solution.py:31
  11.4 469.3 %all-gather.9.cloned.1.call-start = ((), (), s32[]{:S(2)}) async-start(), calls=%async_computation.2 | async-start | bytes 12976128 | tf_op jit(solution)/shard_map/all_gather | solution.py:31
  105.3 119.7 %all-to-all-start.1 = ((bf16[32,384,128]{2,1,0:T(8,128)(2,1)}), bf16[32,384,128]{2,1,0:T(8,128)(2,1)S(1)}, u32[]{:S(2)}, u32[]{:S(2)}) async-start(bf16[32,384,128]{2,1,0:T(8,128)(2,1)} %bitcast.37), calls=%async_computation.1 | async-start | bytes 6291456 | tf_op jit(solution)/shard_map/all_to_all | solution.py:29
  225.0 5.8 %copy-start = (s32[12,3]{0,1:T(4,128)S(1)}, s32[12,3]{0,1:T(4,128)}, u32[]{:S(2)}) copy-start(s32[12,3]{0,1:T(4,128)} %param.5) | copy-start | bytes 436
  225.0 108.7 %all-to-all-start = ((bf16[32,384,128]{2,1,0:T(8,128)(2,1)}), bf16[32,384,128]{2,1,0:T(8,128)(2,1)}, u32[]{:S(2)}, u32[]{:S(2)}) async-start(bf16[32,384,128]{2,1,0:T(8,128)(2,1)} %bitcast.36), calls=%async_computation | async-start | bytes 6291456 | tf_op jit(solution)/shard_map/all_to_all | solution.py:29
Sparse Core Ops, SparseCore 0:
  10.0 95.2 all-gather.14
  107.9 107.4 all-gather.10
  217.2 157.1 all-gather.12
  376.0 104.6 all-gather.8
where the time goes:
time: 499 us
  waiting for transfers between devices  437 us (88%)
  matrix products  23 us (5%)
  between operations  13.2 us (3%)
  local copies, waits for them, and re-layouts  12.1 us (2%)
  starting transfers between devices  11.5 us (2%)
    all_gather x2, waiting for transfers between devices, shards(): all_pages = lax.all_gather(local_panel, 'row', axis=0, tiled=True)  198 us
    all_gather x2, waiting for transfers between devices, shards(): lax.all_gather(local_panel, 'col', axis=1, tiled=True)  132 us
    all_to_all x2, waiting for transfers between devices, shards(): lax.all_to_all(all_pages, 'col', split_axis=0, concat_axis=1, tiled=True)  105 us
    dot_general x2, matrix products, product_nt(): lax.dot_general(left, right, (((1,), (1,)), ((), ())), preferred_element_...  23 us
    all_to_all x2, starting transfers between devices, shards(): lax.all_to_all(all_pages, 'col', split_axis=0, concat_axis=1, tiled=True)  11.3 us
  transfers between devices with their start and end apart: 6, of which 6 were waited for; matrix products, arithmetic and copies ran while one was open for 5% of the time, Pallas kernels for 0%

commit v1 on v0

--- a/solution.py
+++ b/solution.py
@@ -2,6 +2,7 @@
 import jax.numpy as jnp
 from jax import lax
 from jax.sharding import PartitionSpec as P
+from jax.lax import all_to_all, axis_size
 
 TILE = 128
 SECTIONS = 2
@@ -27,9 +28,18 @@
         local_panel = live_tiles[section]
         all_pages = lax.all_gather(local_panel, "row", axis=0, tiled=True)
         column_block = lax.all_to_all(all_pages, "col", split_axis=0, concat_axis=1, tiled=True)
-        total = total + product_nt(
-            lax.all_gather(local_panel, "col", axis=1, tiled=True), column_block
-        )
+
+        def build_tasks(arr):
+            current_arr = all_to_all(
+                jnp.stack([arr] * axis_size("col"), axis=0),
+                axis_name="col",
+                split_axis=0,
+                concat_axis=0,
+            )
+            block_next = jnp.concatenate(current_arr, axis=1)
+            return block_next
+
+        total = total + product_nt(build_tasks(local_panel), column_block)
     return total * spread_tiles(c_mask).astype(jnp.float32)
 
 

time: 499 us -> 897 us (1.80)
  blocking collectives: 0 us -> 359 us
  waiting for transfers between devices: 437 us -> 470 us
    all_to_all x0 -> x2, blocking collectives: none -> 359 us  [the longest x1 280 us: build_tasks(): all_to_all(jnp.stack([arr] * axis_size('col'), axis=0), axis_name='col',...]
    all_to_all x0 -> x1, waiting for transfers between devices: none -> 260 us  [build_tasks(): all_to_all(jnp.stack([arr] * axis_size('col'), axis=0), axis_name='col',...]
    all_gather x2 -> x0, waiting for transfers between devices: 132 us -> none  [shards(): lax.all_gather(local_panel, 'col', axis=1, tiled=True)]
    all_to_all x2 -> x1, waiting for transfers between devices: 105 us -> 9.64 us  [shards(): lax.all_to_all(all_pages, 'col', split_axis=0, concat_axis=1, tiled=True)]
    another operation x0 -> x2, local copies, waits for them, and re-layouts: none -> 14.8 us  [build_tasks(): jnp.stack([arr] * axis_size('col'), axis=0)]
  transfers between devices with their start and end apart: 6 -> 4, of which waited for: 6 -> 4; matrix products, arithmetic and copies ran while one was open for 5% -> 2% of each run, Pallas kernels for 0% -> 0%
where the time goes in v1:
time: 897 us
  waiting for transfers between devices  470 us (52%)
  blocking collectives  359 us (40%)
  matrix products  23.1 us (3%)
  local copies, waits for them, and re-layouts  18.3 us (2%)
  between operations  13.5 us (2%)
  starting transfers between devices  10.7 us (1%)
    all_to_all x1, blocking collectives, build_tasks(): all_to_all(jnp.stack([arr] * axis_size('col'), axis=0), axis_name='col',...  280 us
    all_to_all x1, waiting for transfers between devices, build_tasks(): all_to_all(jnp.stack([arr] * axis_size('col'), axis=0), axis_name='col',...  260 us
    all_gather x2, waiting for transfers between devices, shards(): all_pages = lax.all_gather(local_panel, 'row', axis=0, tiled=True)  199 us
    all_to_all x1, blocking collectives, shards(): lax.all_to_all(all_pages, 'col', split_axis=0, concat_axis=1, tiled=True)  78.7 us
    dot_general x2, matrix products, product_nt(): lax.dot_general(left, right, (((1,), (1,)), ((), ())), preferred_element_...  23.1 us
  transfers between devices with their start and end apart: 4, of which 4 were waited for; matrix products, arithmetic and copies ran while one was open for 2% of the time, Pallas kernels for 0%

profile of v1, /device:TPU:1, one launch (start us, length us, event | category | flops | bytes accessed | tf_op | source)
XLA Modules:
  0.0 896.6 jit_solution(12164170579112518557)
XLA Ops:
  6.5 0.0 all-gather.7.cloned.1.call-start
  6.5 0.7 convert_element_type.22
  7.2 0.1 broadcast_bitcast_fusion.1
  7.3 1.6 broadcast_multiply_fusion
  8.9 1.1 slice_bitcast_fusion.1
  10.0 0.0 all-gather.7.cloned.1.call-update
  10.1 95.4 %all-gather.7.cloned.1.call-done = bf16[1,12288,128]{2,1,0:T(8,128)(2,1)} async-done(((bf16[1,1536,128]{2,1,0:T(8,128)(2,1)}), bf16[1,12288,128]{2,1,0:T(8,128)(2,1)}) %all-gather.7.cloned.1.call-update) | async-done | bytes 3145744 | tf_op jit(solution)/shard_map/all_gather | solution.py:29
  105.5 5.6 all-to-all-start.3
  111.0 0.0 all-gather.5.cloned.1.call-start
  111.1 0.7 all-gather.5.cloned.1.call-update
  111.8 103.8 %all-gather.5.cloned.1.call-done = bf16[1,12288,128]{2,1,0:T(8,128)(2,1)} async-done(((bf16[1,1536,128]{2,1,0:T(8,128)(2,1)}), bf16[1,12288,128]{2,1,0:T(8,128)(2,1)}) %all-gather.5.cloned.1.call-update) | async-done | bytes 3145744 | tf_op jit(solution)/shard_map/all_gather | solution.py:29
  215.6 9.6 %all-to-all-done.3 = bf16[32,384,128]{2,1,0:T(8,128)(2,1)S(1)} async-done(((bf16[32,384,128]{2,1,0:T(8,128)(2,1)}), bf16[32,384,128]{2,1,0:T(8,128)(2,1)S(1)}, u32[]{:S(2)}, u32[]{:S(2)}) %all-to-all-start.3) | async-done | bytes 3145760 | tf_op jit(solution)/shard_map/all_to_all | solution.py:30
  225.2 0.0 copy-start
  225.2 0.0 copy-start.2
  225.2 78.7 %all_to_all.42 = bf16[32,384,128]{2,1,0:T(8,128)(2,1)} all-to-all(bf16[32,384,128]{2,1,0:T(8,128)(2,1)} %bitcast.60), channel_id=1, replica_groups=mesh['row'=8,'col'=32] {'col'}, dimensions={0} | all-to-all | bytes 6291456 | tf_op jit(solution)/shard_map/all_to_all | solution.py:30
  303.9 0.0 copy-done
  303.9 0.0 copy-done.2
  303.9 7.4 stack.7
  311.3 280.2 %all_to_all.43 = bf16[32,1536,128]{2,1,0:T(8,128)(2,1)} all-to-all(bf16[32,1536,128]{2,1,0:T(8,128)(2,1)} %stack.7), channel_id=1, replica_groups=mesh['row'=8,'col'=32] {'col'}, dimensions={0} | all-to-all | bytes 25165824 | tf_op jit(solution)/shard_map/all_to_all | solution.py:33
  591.5 7.4 stack.6
  598.9 0.0 copy-start.3
  598.9 5.1 all-to-all-start
  604.0 0.0 copy-done.3
  604.0 0.1 broadcast_bitcast_fusion
  604.1 0.3 broadcast_in_dim.12
  604.4 2.0 copy.5
  606.3 0.0 copy-start.1
  606.3 11.7 %fusion.21 = f32[1536,384]{1,0:T(8,128)} fusion(bf16[32,384,128]{2,1,0:T(8,128)(2,1)} %copy-done, bf16[32,1536,128]{2,1,0:T(8,128)(2,1)} %all_to_all.43), kind=kOutput, calls=%fused_computation.9 | convolution fusion | flops 4831838208 | bytes 18087936 | tf_op jit(solution)/shard_map/dot_general | solution.py:17
  618.1 260.3 %all-to-all-done = bf16[32,1536,128]{2,1,0:T(8,128)(2,1)} async-done(((bf16[32,1536,128]{2,1,0:T(8,128)(2,1)}), bf16[32,1536,128]{2,1,0:T(8,128)(2,1)}, u32[]{:S(2)}, u32[]{:S(2)}) %all-to-all-start) | async-done | bytes 12582944 | tf_op jit(solution)/shard_map/all_to_all | solution.py:33
  878.4 0.0 copy-done.1
  878.4 11.4 %fusion.16 = f32[1536,384]{1,0:T(8,128)} fusion(f32[1536,384]{1,0:T(8,128)} %copy.5, f32[1536,384]{1,0:T(8,128)} %fusion.21, bf16[32,384,128]{2,1,0:T(8,128)(2,1)S(1)} %copy-done.1, bf16[32,1536,128]{2,1,0:T(8,128)(2,1)} %all-to-all-done), kind=kOutput, calls=%fused_computation.8 | convolution fusion | flops 4833017856 | bytes 22806528 | tf_op jit(solution)/shard_map/dot_general | solution.py:17
  (4 shorter events, 0.0 us)
Async XLA Ops:
  6.5 98.9 %all-gather.7.cloned.1.call-start = ((), (), s32[]{:S(2)}) async-start(), calls=%async_computation.5 | async-start | bytes 3538944 | tf_op jit(solution)/shard_map/all_gather | solution.py:29
  105.5 119.7 %all-to-all-start.3 = ((bf16[32,384,128]{2,1,0:T(8,128)(2,1)}), bf16[32,384,128]{2,1,0:T(8,128)(2,1)S(1)}, u32[]{:S(2)}, u32[]{:S(2)}) async-start(bf16[32,384,128]{2,1,0:T(8,128)(2,1)} %bitcast.59), calls=%async_computation.3 | async-start | bytes 6291456 | tf_op jit(solution)/shard_map/all_to_all | solution.py:30
  111.0 104.5 %all-gather.5.cloned.1.call-start = ((), (), s32[]{:S(2)}) async-start(), calls=%async_computation.4 | async-start | bytes 3538944 | tf_op jit(solution)/shard_map/all_gather | solution.py:29
  225.2 78.7 %copy-start = (bf16[32,384,128]{2,1,0:T(8,128)(2,1)}, bf16[32,384,128]{2,1,0:T(8,128)(2,1)S(1)}, u32[]{:S(2)}) copy-start(bf16[32,384,128]{2,1,0:T(8,128)(2,1)S(1)} %all-to-all-done.3) | copy-start | bytes 9437188
  225.2 78.7 %copy-start.2 = (bf16[1536,128]{1,0:T(8,128)(2,1)S(1)}, bf16[1536,128]{1,0:T(8,128)(2,1)}, u32[]{:S(2)}) copy-start(bf16[1536,128]{1,0:T(8,128)(2,1)} %get-tuple-element.6) | copy-start | bytes 1179652
  598.9 5.1 copy-start.3
  598.9 279.4 %all-to-all-start = ((bf16[32,1536,128]{2,1,0:T(8,128)(2,1)}), bf16[32,1536,128]{2,1,0:T(8,128)(2,1)}, u32[]{:S(2)}, u32[]{:S(2)}) async-start(bf16[32,1536,128]{2,1,0:T(8,128)(2,1)} %stack.6), calls=%async_computation | async-start | bytes 25165824 | tf_op jit(solution)/shard_map/all_to_all | solution.py:33
  606.3 272.0 %copy-start.1 = (bf16[32,384,128]{2,1,0:T(8,128)(2,1)S(1)}, bf16[32,384,128]{2,1,0:T(8,128)(2,1)}, u32[]{:S(2)}) copy-start(bf16[32,384,128]{2,1,0:T(8,128)(2,1)} %all_to_all.42) | copy-start | bytes 9437188
Sparse Core Ops, SparseCore 0:
  10.2 95.2 all-gather.6
  114.5 101.0 all-gather.4
